TPU v7x, 32 devices: a whole 2x2x4 slice. The times are simulated.
32 devices in a mesh: ctx: 8 (over z, x), head: 4 (over y, core).
Axes of the slice: x: 2, y: 2, z: 4, core: 2. Of those that a mesh axis runs over, the one named last changes fastest.
Arguments:
- queries: bfloat16 [16384, 2048], P('ctx', 'head'), may hold values from -6 to 6
- keys: bfloat16 [16384, 2048], P('ctx', 'head'), may hold values from -6 to 6
- values: bfloat16 [16384, 4096], P('ctx', 'head'), may hold values from -6 to 6
- gate_pre: float32 [2, 8, 16384], P(None, None, ('ctx', 'head')), may hold values from -8 to 320
Outputs:
- hidden: bfloat16 [16384, 4096], P('ctx', 'head')
- closing_memory: float32 [8, 256, 512], P('head', 'ctx')
- final_norm: float32 [8, 256], P('head')
- final_max: float32 [8], P('head')
All inputs are finite; a program needn't handle non-finite values.
Results may differ from a plain program's by a relative error of at most 0.004.
Values sent between devices are 32-bit elements; how exact they have to be, the bound alone decides.
A program may use at most 128 MiB of HBM per device.

v0:
```python
import jax
import jax.numpy as jnp
from jax import lax
from jax.sharding import PartitionSpec as P

DQK = 256
BLK = 512


NEG = -1e30


def prefix(part, axis, combine, identity, reverse):
    count = lax.axis_size(axis)
    place = lax.axis_index(axis)
    ahead = count - 1 - place if reverse else place
    gathered = jax.tree.map(lambda a: lax.all_gather(a, axis), part)
    state = jax.tree.map(lambda a, e: jnp.zeros_like(a) + jnp.asarray(e, a.dtype), part, identity)

    def one(lap, state):
        source = count - 1 - lap if reverse else lap
        return combine(
            state, jax.tree.map(lambda a: lax.dynamic_index_in_dim(a, source, 0, False), gathered)
        )

    return lax.fori_loop(0, ahead, one, state)


def block_step(carry, inputs):
    memory, normal, stab, offset = carry
    q_block, key_block, v_block, in_gate, forget = inputs
    length = q_block.shape[0]
    scale = q_block.shape[1] ** (-0.5)
    log_forget = jax.nn.log_sigmoid(forget)
    cum = jnp.cumsum(log_forget)
    whole = cum[-1]
    places = jnp.arange(length, dtype=jnp.int32)
    causal = places[:, None] >= places[None, :]
    log_weight = jnp.where(causal, cum[:, None] - cum[None, :] + in_gate[None, :], NEG)
    top = jnp.maximum(cum + stab, jnp.max(log_weight, axis=1))
    weights = jnp.where(causal, jnp.exp(log_weight - top[:, None]), 0.0)
    scores = jnp.dot(q_block, key_block.T, preferred_element_type=jnp.float32) * scale
    mixed = weights * scores
    denom = jnp.sum(mixed, axis=1)
    numer = jnp.dot(mixed.astype(jnp.bfloat16), v_block, preferred_element_type=jnp.float32)
    carried = jnp.exp(cum + stab - top)
    q_float = q_block.astype(jnp.float32)
    numer = numer + carried[:, None] * jnp.dot(q_float, memory, precision=lax.Precision.HIGHEST)
    denom = denom + carried * jnp.dot(q_float, normal, precision=lax.Precision.HIGHEST)
    new_stab = jnp.maximum(whole + stab, jnp.max(whole - cum + in_gate))
    keep = jnp.exp(whole + stab - new_stab)
    taken = jnp.exp(whole - cum + in_gate - new_stab)
    k_float = key_block.astype(jnp.float32) * scale * taken[:, None]
    memory = keep * memory + jnp.dot(
        k_float.T, v_block.astype(jnp.float32), precision=lax.Precision.HIGHEST
    )
    normal = keep * normal + jnp.sum(k_float, axis=0)
    return ((memory, normal, new_stab, offset + whole), (numer, denom, top, cum + offset))


def local_chain(q_head, k_head, v_head, in_gate, forget):
    count = q_head.shape[0] // BLK
    width = v_head.shape[1]
    blocks = (
        q_head.reshape(count, BLK, DQK),
        k_head.reshape(count, BLK, DQK),
        v_head.reshape(count, BLK, width),
        in_gate.reshape(count, BLK),
        forget.reshape(count, BLK),
    )
    start = (
        jnp.zeros((DQK, width), jnp.float32),
        jnp.zeros((DQK,), jnp.float32),
        jnp.full((), NEG, jnp.float32),
        jnp.zeros((), jnp.float32),
    )
    final, outs = lax.scan(block_step, start, blocks)
    numer, denom, top, cum = outs
    row_entries = q_head.shape[0]
    return (
        numer.reshape(row_entries, width),
        denom.reshape(row_entries),
        top.reshape(row_entries),
        cum.reshape(row_entries),
        final[0],
        final[1],
        final[2],
        final[3],
    )


def chain(early, late):
    early_mem, early_norm, early_stab, early_log = early
    late_mem, late_norm, late_stab, late_log = late
    shifted = early_stab + late_log
    peak = jnp.maximum(shifted, late_stab)
    early_factor = jnp.exp(shifted - peak)
    late_factor = jnp.exp(late_stab - peak)
    merged_mem = early_factor[:, None, None] * early_mem + late_factor[:, None, None] * late_mem
    merged_norm = early_factor[:, None] * early_norm + late_factor[:, None] * late_norm
    return (merged_mem, merged_norm, peak, early_log + late_log)


def plus(early, late):
    return early + late


def on_device(queries, keys, values, gate_pre):
    toks = queries.shape[0]
    heads_here = queries.shape[1] // DQK
    width = values.shape[1] // heads_here
    gates = lax.all_to_all(gate_pre, "head", split_axis=1, concat_axis=2, tiled=True)
    q_three = queries.reshape(toks, heads_here, DQK)
    k_three = keys.reshape(toks, heads_here, DQK)
    v_three = values.reshape(toks, heads_here, width)
    numer, denom, top, cum, memory, normal, stab, total = jax.vmap(
        local_chain, in_axes=(1, 1, 1, 0, 0)
    )(q_three, k_three, v_three, gates[0], gates[1])
    zero_heads = jnp.zeros((heads_here,), jnp.float32)
    identity = (
        jnp.zeros_like(memory),
        jnp.zeros_like(normal),
        jnp.full((heads_here,), NEG, jnp.float32),
        zero_heads,
    )
    in_mem, in_norm, in_stab, in_log = prefix(
        (memory, normal, stab, total), "ctx", chain, identity, False
    )
    reach = cum + in_stab[:, None]
    peak_all = jnp.maximum(reach, top)
    local_factor = jnp.exp(top - peak_all)
    carried = jnp.exp(reach - peak_all)
    q_float = q_three.astype(jnp.float32)
    from_memory = jnp.einsum("thd,hde->hte", q_float, in_mem, precision=lax.Precision.HIGHEST)
    from_norm = jnp.einsum("thd,hd->ht", q_float, in_norm, precision=lax.Precision.HIGHEST)
    numer = numer * local_factor[..., None] + carried[..., None] * from_memory
    denom = denom * local_factor + carried * from_norm
    result = (numer / jnp.maximum(jnp.abs(denom), 1.0)[..., None]).astype(jnp.bfloat16)
    hidden = result.transpose(1, 0, 2).reshape(toks, heads_here * width)
    after = prefix(total, "ctx", plus, zero_heads, True)
    at_end = stab + after
    final_max = lax.pmax(at_end, "ctx")
    factor = jnp.exp(at_end - final_max)
    closing_memory = lax.psum_scatter(
        memory * factor[:, None, None], "ctx", scatter_dimension=1, tiled=True
    )
    final_norm = lax.psum(normal * factor[:, None], "ctx")
    return (hidden, closing_memory, final_norm, final_max)


def solution(mesh):
    in_specs = (
        P("ctx", "head"),
        P("ctx", "head"),
        P("ctx", "head"),
        P(None, None, ("ctx", "head")),
    )
    out_specs = (P("ctx", "head"), P("head", "ctx", None), P("head", None), P("head"))
    return jax.shard_map(
        on_device, mesh=mesh, in_specs=in_specs, out_specs=out_specs, check_vma=False
    )
```

profile of v0, /device:TPU:0, one launch (start us, length us, event | category | flops | bytes accessed | tf_op | source)
XLA Modules:
  0.0 305.8 jit_solution(2923703625764490587)
XLA Ops:
  7.2 1.4 copy.39
  8.6 4.2 %all-to-all-start = ((f32[2,8,512]{2,0,1:T(2,128)}), f32[2,8,512]{2,0,1:T(2,128)S(1)}, u32[]{:S(2)}, u32[]{:S(2)}) async-start(f32[2,8,512]{2,0,1:T(2,128)} %copy.39), calls=%async_computation | async-start | bytes 65536 | tf_op jit(solution)/shard_map/all_to_all | solution.py:112
  12.9 4.0 %copy.45 = bf16[2048,512]{0,1:T(8,128)(2,1)} copy(bf16[2048,512]{1,0:T(8,128)(2,1)} %param.10) | data formatting | bytes 4194304 | tf_op args[0]
  16.8 2.8 copy.46
  19.7 6.4 %copy.43 = bf16[2048,1024]{0,1:T(8,128)(2,1)} copy(bf16[2048,1024]{1,0:T(8,128)(2,1)} %param.12) | data formatting | bytes 8388608 | tf_op args[2]
  26.1 6.2 %copy.44 = bf16[2,2048,512]{2,1,0:T(8,128)(2,1)} copy(bf16[2,2048,512]{1,2,0:T(8,128)(2,1)} %bitcast.202) | data formatting | bytes 8388608 | tf_op jit(solution)/shard_map/vmap()/transpose | solution.py:67
  32.3 3.9 %copy.41 = bf16[2048,512]{0,1:T(8,128)(2,1)} copy(bf16[2048,512]{1,0:T(8,128)(2,1)} %param.11) | data formatting | bytes 4194304 | tf_op args[1]
  36.2 4.0 %copy.42 = bf16[2,2048,256]{2,1,0:T(8,128)(2,1)} copy(bf16[2,2048,256]{1,2,0:T(8,128)(2,1)} %bitcast.204) | data formatting | bytes 4194304 | tf_op jit(solution)/shard_map/vmap()/transpose | solution.py:66
  40.2 63.6 %while.55 = (s32[]{:T(128)}, f32[2,256,512]{2,1,0:T(8,128)S(1)}, f32[2,256]{1,0:T(2,128)S(1)}, f32[2]{0:T(128)S(1)}, f32[2]{0:T(128)S(1)}, /*index=5*/f32[4,2,51...) while((s32[]{:T(128)}, f32[2,256,512]{2,1,0:T(8,128)S(1)}, ...), condition=%wide.region_7.8_spmd.clone, body=%wide.region_0.7_spmd.clone.sunk | while | flops 4040316928 | bytes 34551896 | solution.py:77
  40.3 0.6 reduce-window.14
  41.6 0.2 fusion.91
  41.8 0.4 fusion.95
  42.3 2.1 fusion.96
  44.5 2.0 fusion.97
  46.6 1.3 fusion.93
  47.9 1.5 fusion.98
  49.6 3.6 %bitcast_dynamic-update-slice_fusion.3 = f32[4,2,512,512]{3,2,1,0:T(8,128)} fusion(f32[4,2,512,512]{3,2,1,0:T(8,128)} %get-tuple-element.641, s32[]{:T(128)} %get-tuple-element.636, f32[2,512,512]{2,1,0:T(8,128)S(1)} %fusion.97, f32[2,512]{1,0:T(2,128)S(1)} %get-tuple-element.615, f32[2,256,512]{2,1,0:T(8,128)S(1)} %get-tuple-element.637, ...), kind=kOutput, calls=%fused_computation.13.clone.1 | convolution fusion | flops 1611923456 | bytes 5772289 | tf_op jit(solution)/shard_map/vmap()/while/body/eval_jaxpr/dot_general | solution.py:48
  53.2 3.0 convolution_add_fusion.2
  56.3 0.6 reduce-window.14
  57.5 0.2 fusion.91
  57.8 0.4 fusion.95
  58.3 2.1 fusion.96
  60.4 2.0 fusion.97
  62.5 1.3 fusion.93
  63.9 1.5 fusion.98
  65.6 3.5 %bitcast_dynamic-update-slice_fusion.3 = f32[4,2,512,512]{3,2,1,0:T(8,128)} fusion(f32[4,2,512,512]{3,2,1,0:T(8,128)} %get-tuple-element.641, s32[]{:T(128)} %get-tuple-element.636, f32[2,512,512]{2,1,0:T(8,128)S(1)} %fusion.97, f32[2,512]{1,0:T(2,128)S(1)} %get-tuple-element.615, f32[2,256,512]{2,1,0:T(8,128)S(1)} %get-tuple-element.637, ...), kind=kOutput, calls=%fused_computation.13.clone.1 | convolution fusion | flops 1611923456 | bytes 5772289 | tf_op jit(solution)/shard_map/vmap()/while/body/eval_jaxpr/dot_general | solution.py:48
  69.1 3.0 convolution_add_fusion.2
  72.1 0.6 reduce-window.14
  73.4 0.2 fusion.91
  73.6 0.4 fusion.95
  74.2 2.1 fusion.96
  76.3 2.0 fusion.97
  78.4 1.3 fusion.93
  79.7 1.5 fusion.98
  81.5 3.5 %bitcast_dynamic-update-slice_fusion.3 = f32[4,2,512,512]{3,2,1,0:T(8,128)} fusion(f32[4,2,512,512]{3,2,1,0:T(8,128)} %get-tuple-element.641, s32[]{:T(128)} %get-tuple-element.636, f32[2,512,512]{2,1,0:T(8,128)S(1)} %fusion.97, f32[2,512]{1,0:T(2,128)S(1)} %get-tuple-element.615, f32[2,256,512]{2,1,0:T(8,128)S(1)} %get-tuple-element.637, ...), kind=kOutput, calls=%fused_computation.13.clone.1 | convolution fusion | flops 1611923456 | bytes 5772289 | tf_op jit(solution)/shard_map/vmap()/while/body/eval_jaxpr/dot_general | solution.py:48
  85.0 3.0 convolution_add_fusion.2
  88.1 0.6 reduce-window.14
  89.3 0.2 fusion.91
  89.6 0.4 fusion.95
  90.1 2.1 fusion.96
  92.2 2.0 fusion.97
  94.3 1.3 fusion.93
  95.7 1.5 fusion.98
  97.4 3.5 %bitcast_dynamic-update-slice_fusion.3 = f32[4,2,512,512]{3,2,1,0:T(8,128)} fusion(f32[4,2,512,512]{3,2,1,0:T(8,128)} %get-tuple-element.641, s32[]{:T(128)} %get-tuple-element.636, f32[2,512,512]{2,1,0:T(8,128)S(1)} %fusion.97, f32[2,512]{1,0:T(2,128)S(1)} %get-tuple-element.615, f32[2,256,512]{2,1,0:T(8,128)S(1)} %get-tuple-element.637, ...), kind=kOutput, calls=%fused_computation.13.clone.1 | convolution fusion | flops 1611923456 | bytes 5772289 | tf_op jit(solution)/shard_map/vmap()/while/body/eval_jaxpr/dot_general | solution.py:48
  100.9 3.0 convolution_add_fusion.2
  103.9 1.0 copy-done
  105.0 0.6 dynamic-slice
  106.2 0.2 dynamic-update-slice
  106.4 22.6 %all-reduce = f32[16]{0:T(128)S(1)} all-reduce(f32[16]{0:T(128)S(1)} %dynamic-update-slice), channel_id=2, replica_groups=mesh['ctx'=8,'head'=4] {'ctx'}, use_global_device_ids=true, to_apply=%add | all-reduce | flops 16 | bytes 128
  129.1 0.3 while.54
  129.4 17.8 %pmax.7 = f32[2]{0:T(128)S(1)} all-reduce(f32[2]{0:T(128)S(1)} %add.167), channel_id=1, replica_groups=mesh['ctx'=8,'head'=4] {'ctx'}, use_global_device_ids=true, to_apply=%region_12.13 | all-reduce | flops 2 | bytes 16 | tf_op jit(solution)/shard_map/pmax | solution.py:142
  147.3 0.2 dynamic-update-slice.1
  147.6 19.7 %all-reduce.2 = (f32[16]{0:T(128)S(1)}, f32[2,256]{1,0:T(2,128)}) all-reduce(f32[16]{0:T(128)S(1)} %dynamic-update-slice.1, f32[2,256]{1,0:T(2,128)S(1)} %broadcast_multiply_fusion.1), channel_id=3, replica_groups=mesh['ctx'=8,'head'=4] {'ctx'}, use_global_device_ids=true, to_apply=%add.1 | all-reduce | flops 528 | bytes 4224
  167.3 10.4 %copy.50 = f32[2,4,512,512]{2,1,3,0:T(4,128)} copy(f32[2,4,512,512]{3,2,0,1:T(8,128)} %bitcast.203) | data formatting | bytes 16777216 | tf_op jit(solution)/shard_map/vmap()/transpose | solution.py:81
  177.8 11.0 %reshape.314 = f32[2,2048,512]{1,2,0:T(8,128)} reshape(f32[2,4,512,512]{2,1,3,0:T(4,128)} %copy.50) | data formatting | bytes 16777216 | tf_op jit(solution)/shard_map/vmap()/reshape | solution.py:81
  188.7 26.5 %all-gather.4 = f32[8,2,256]{2,1,0:T(2,128)S(1)} all-gather(f32[1,2,256]{2,1,0:T(2,128)S(1)} %bitcast.215), channel_id=5, replica_groups=mesh['ctx'=8,'head'=4] {'ctx'}, dimensions={0}, use_global_device_ids=true | all-gather | bytes 18432 | tf_op jit(solution)/shard_map/all_gather | solution.py:17
  215.3 1.2 broadcast_multiply_fusion
  216.5 16.7 %all-gather.7.cloned.1.call-done = f32[16,256,512]{2,1,0:T(8,128)} async-done(((f32[2,256,512]{2,1,0:T(8,128)}), f32[16,256,512]{2,1,0:T(8,128)}) %all-gather.7.cloned.1.call-update) | async-done | bytes 8388624 | tf_op jit(solution)/shard_map/all_gather | solution.py:17
  233.4 0.2 while.53
  233.6 1.4 copy-done.4
  234.9 0.9 fusion.47
  236.0 8.3 %fusion.41 = bf16[2,2048,512]{1,2,0:T(8,128)(2,1)} fusion(f32[2,2048,512]{1,2,0:T(8,128)} %reshape.314, f32[2,256,512]{2,1,0:T(8,128)S(1)} %get-tuple-element.221, bf16[2048,2,256]{0,2,1:T(8,128)(2,1)S(1)} %bitcast.201, f32[2,2048]{1,0:T(2,128)S(1)} %get-tuple-element.397, f32[2,2048]{1,0:T(2,128)S(1)} %get-tuple-element.399, ...), kind=kOutput, calls=%fused_computation.75 | convolution fusion | flops 6452936704 | bytes 15777792 | tf_op jit(solution)/shard_map/thd,hde->hte/dot_general | solution.py:134
  244.3 6.4 %copy.53 = bf16[2048,1024]{1,0:T(8,128)(2,1)} copy(bf16[2048,1024]{0,1:T(8,128)(2,1)} %bitcast.205) | data formatting | bytes 8388608
  250.7 48.3 %reduce-scatter.2.cloned.1.call-done = f32[2,32,512]{2,1,0:T(8,128)} async-done(((f32[2,256,512]{2,1,0:T(8,128)}), f32[2,32,512]{2,1,0:T(8,128)}) %reduce-scatter.2.cloned.1.call-update) | async-done | bytes 131088 | tf_op jit(solution)/shard_map/reduce_scatter | solution.py:144
  (126 shorter events, 5.4 us)
Async XLA Ops:
  8.6 31.6 %all-to-all-start = ((f32[2,8,512]{2,0,1:T(2,128)}), f32[2,8,512]{2,0,1:T(2,128)S(1)}, u32[]{:S(2)}, u32[]{:S(2)}) async-start(f32[2,8,512]{2,0,1:T(2,128)} %copy.39), calls=%async_computation | async-start | bytes 65536 | tf_op jit(solution)/shard_map/all_to_all | solution.py:112
  12.8 220.4 %all-gather.7.cloned.1.call-start = ((), (), s32[]{:S(2)}) async-start(), calls=%async_computation.3 | async-start | bytes 9437184 | tf_op jit(solution)/shard_map/all_gather | solution.py:17
  40.2 64.7 %copy-start.5 = (u32[32]{0:T(128)S(1)}, u32[32]{0:T(128)}, u32[]{:S(2)}) copy-start(u32[32]{0:T(128)} %constant.101) | copy-start | bytes 388
  40.2 4.2 %copy-start.2 = (bf16[4,2,512,256]{3,2,0,1:T(8,128)(2,1)}, bf16[4,2,512,256]{3,2,0,1:T(8,128)(2,1)S(1)}, u32[]{:S(2)}) copy-start(bf16[4,2,512,256]{3,2,0,1:T(8,128)(2,1)S(1)} %get-tuple-element.666) | copy-start | bytes 6291460 | tf_op jit(solution)/shard_map/vmap()/while
  53.2 3.0 copy-start.3
  56.2 4.2 %copy-start.2 = (bf16[4,2,512,256]{3,2,0,1:T(8,128)(2,1)}, bf16[4,2,512,256]{3,2,0,1:T(8,128)(2,1)S(1)}, u32[]{:S(2)}) copy-start(bf16[4,2,512,256]{3,2,0,1:T(8,128)(2,1)S(1)} %get-tuple-element.666) | copy-start | bytes 6291460 | tf_op jit(solution)/shard_map/vmap()/while
  69.1 3.0 copy-start.3
  72.1 4.2 %copy-start.2 = (bf16[4,2,512,256]{3,2,0,1:T(8,128)(2,1)}, bf16[4,2,512,256]{3,2,0,1:T(8,128)(2,1)S(1)}, u32[]{:S(2)}) copy-start(bf16[4,2,512,256]{3,2,0,1:T(8,128)(2,1)S(1)} %get-tuple-element.666) | copy-start | bytes 6291460 | tf_op jit(solution)/shard_map/vmap()/while
  85.0 3.0 copy-start.3
  88.0 4.2 %copy-start.2 = (bf16[4,2,512,256]{3,2,0,1:T(8,128)(2,1)}, bf16[4,2,512,256]{3,2,0,1:T(8,128)(2,1)S(1)}, u32[]{:S(2)}) copy-start(bf16[4,2,512,256]{3,2,0,1:T(8,128)(2,1)S(1)} %get-tuple-element.666) | copy-start | bytes 6291460 | tf_op jit(solution)/shard_map/vmap()/while
  100.9 3.0 copy-start.3
  103.9 1.0 copy-start
  104.9 194.0 %reduce-scatter.2.cloned.1.call-start = ((), (), s32[]{:S(2)}) async-start(), calls=%async_computation.2 | async-start | bytes 1179648 | tf_op jit(solution)/shard_map/reduce_scatter | solution.py:144
  147.2 30.5 %copy-start.6 = (f32[2]{0:T(128)}, f32[2]{0:T(128)S(1)}, u32[]{:S(2)}) copy-start(f32[2]{0:T(128)S(1)} %pmax.7) | copy-start | bytes 28
  177.8 37.5 %copy-start.1 = (f32[2,256,512]{2,1,0:T(8,128)S(1)}, f32[2,256,512]{2,1,0:T(8,128)}, u32[]{:S(2)}) copy-start(f32[2,256,512]{2,1,0:T(8,128)} %copy-done) | copy-start | bytes 3145732
  233.4 1.6 copy-start.4
Sparse Core Ops, SparseCore 0:
  105.0 128.1 all-gather.6
  237.2 61.6 reduce-scatter.1
where the time goes:
time: 308 us; the launch traced here: 306 us
  blocking collectives  86.7 us (28%)
  waiting for transfers between devices  65 us (21%)
  local copies, waits for them, and re-layouts  61.8 us (20%)
  matrix products  57.7 us (19%)
  between operations  14.9 us (5%)
  other arithmetic  14.6 us (5%)
  starting transfers between devices  4.28 us (1%)
    reduce_scatter x1, waiting for transfers between devices, on_device(): lax.psum_scatter(memory * factor[:, None, None], 'ctx', scatter_dimension...  48.3 us
    unnamed x2, blocking collectives  42.3 us
    all_gather x1, blocking collectives, prefix(): gathered = jax.tree.map(lambda a: lax.all_gather(a, axis), part)  26.5 us
    unnamed x20, local copies, waits for them, and re-layouts  25.5 us
    pmax x1, blocking collectives, on_device(): final_max = lax.pmax(at_end, 'ctx')  17.8 us
    all_gather x1, waiting for transfers between devices, prefix(): gathered = jax.tree.map(lambda a: lax.all_gather(a, axis), part)  16.7 us
    dot_general x4, matrix products, block_step(): jnp.dot(q_float, memory, precision=lax.Precision.HIGHEST)  14.1 us
    dot_general x4, matrix products, block_step(): jnp.dot(k_float.T, v_block.astype(jnp.float32), precision=lax.Precision.H...  11.9 us
  transfers between devices with their start and end apart: 3, of which 2 were waited for; matrix products, arithmetic and copies ran while one was open for 22% of the time, Pallas kernels for 0%

commit v1 on v0

v1 whole, which is shorter than its diff:
```python
import functools

import jax
import jax.numpy as jnp
from jax import lax
from jax.experimental import pallas as pl
from jax.experimental.pallas import tpu as pltpu
from jax.sharding import PartitionSpec as P

NEG = -1e30
CW = 128
MESH = pl.DeviceIdType.MESH
F32 = jnp.float32
BF16 = jnp.bfloat16


def shifted(v, k, lane, fill):
    return jnp.where(lane >= k, pltpu.roll(v, k, axis=1), fill)


def kernel(
    nc, nh, hh, toks, dqk, dv,
    q_hbm, k_hbm, v_hbm, g_hbm,
    out_hbm, clos_out, norm_out, max_out,
    q_v, k_v, v_v, g_v, gsend, grecv, ig_s, fg_s,
    a3, mcolb, w3, slp3, insr3, sg3, ng3, norm8, mst, st, norm_st,
    summ, fac, sbuf, srecv, erecv, eout, xsend, xrecv, own, closb, inm,
    numn, cinb, outb,
    in_sem, gs_sem, gr_sem, ss_sem, sr_sem, xs_sem, xr_sem,
    es_sem, er_sem, fs_sem, fr_sem, cs_sem, cr_sem, out_sem,
):
    c = lax.axis_index("ctx")
    hd = lax.axis_index("head")
    i = c // 2
    x = c - 2 * i
    pairs = nc // 2
    L = toks // nh
    R = dqk // nc
    cph = dv // CW
    nu = hh * cph
    nt = hh * nh
    scale = dqk ** (-0.5)

    g_copy = pltpu.make_async_copy(g_hbm, g_v, in_sem.at[0])
    g_copy.start()
    loads = []
    for h in range(hh):
        kc = pltpu.make_async_copy(
            k_hbm.at[:, h * dqk:(h + 1) * dqk], k_v.at[h], in_sem.at[1 + 3 * h])
        vc = pltpu.make_async_copy(
            v_hbm.at[:, h * dv:(h + 1) * dv], v_v.at[h], in_sem.at[2 + 3 * h])
        qc = pltpu.make_async_copy(
            q_hbm.at[:, h * dqk:(h + 1) * dqk], q_v.at[h], in_sem.at[3 + 3 * h])
        loads.append((kc, vc, qc))
    for h in range(hh):
        loads[h][0].start()
        loads[h][1].start()
    for h in range(hh):
        loads[h][2].start()

    barrier = pltpu.get_barrier_semaphore()
    for d in range(1, nh):
        pl.semaphore_signal(barrier, inc=1, device_id=(c, lax.rem(hd + d, nh)), device_id_type=MESH)
    for d in range(1, nc):
        pl.semaphore_signal(barrier, inc=1, device_id=(lax.rem(c + d, nc), hd), device_id_type=MESH)
    g_copy.wait()
    for p in range(nh):
        gsend[p, 0:hh, :] = g_v[0, p * hh:(p + 1) * hh, :]
        gsend[p, hh:2 * hh, :] = g_v[1, p * hh:(p + 1) * hh, :]
    pl.semaphore_wait(barrier, nh - 1 + nc - 1)

    def gate_copy(d):
        to = lax.rem(hd + d, nh)
        return pltpu.make_async_remote_copy(
            src_ref=gsend.at[to], dst_ref=grecv.at[hd], send_sem=gs_sem.at[d],
            recv_sem=gr_sem.at[d], device_id=(c, to), device_id_type=MESH)

    def gate_wait(d):
        frm = lax.rem(hd + nh - d, nh)
        return pltpu.make_async_remote_copy(
            src_ref=gsend.at[frm], dst_ref=grecv.at[frm], send_sem=gs_sem.at[d],
            recv_sem=gr_sem.at[d], device_id=(c, frm), device_id_type=MESH)

    for d in range(1, nh):
        gate_copy(d).start()
    grecv[hd] = gsend[hd]
    for d in range(1, nh):
        gate_wait(d).wait_recv()
    for p in range(nh):
        ig_s[p * hh:(p + 1) * hh, :] = grecv[p, 0:hh, :]
        fg_s[p * hh:(p + 1) * hh, :] = grecv[p, hh:2 * hh, :]
    ig = ig_s[...]
    fg = fg_s[...]
    logf = jnp.minimum(fg, 0.0) - jnp.log1p(jnp.exp(-jnp.abs(fg)))
    lane = lax.broadcasted_iota(jnp.int32, (nt, L), 1)
    cum = logf
    k = 1
    while k < L:
        cum = cum + shifted(cum, k, lane, 0.0)
        k *= 2
    a = ig - cum
    amax_run = a
    k = 1
    while k < L:
        amax_run = jnp.maximum(amax_run, shifted(amax_run, k, lane, NEG))
        k *= 2
    gb = jnp.broadcast_to(cum[:, L - 1:L], (nt, 128))
    ab = jnp.broadcast_to(amax_run[:, L - 1:L], (nt, 128))
    sl = jnp.full((hh, 128), NEG, F32)
    cg = jnp.zeros((hh, 128), F32)
    before, after, gone, keep = [], [], [], []
    for j in range(nh):
        gj = gb[j * hh:(j + 1) * hh]
        new = gj + jnp.maximum(sl, ab[j * hh:(j + 1) * hh])
        before.append(sl)
        gone.append(cg)
        keep.append(jnp.exp(gj + sl - new))
        sl = new
        cg = cg + gj
        after.append(sl)
    slp8 = jnp.concatenate(before, axis=0)
    cg8 = jnp.concatenate(gone, axis=0)
    w = jnp.exp(a + (gb - jnp.concatenate(after, axis=0))[:, 0:1]) * scale
    for r in range(nt):
        a3[r] = a[r:r + 1, :]
        w3[r] = w[r:r + 1, :]
        slp3[r] = slp8[r:r + 1, :]

    def s_copy(u):
        return pltpu.make_async_remote_copy(
            src_ref=sbuf.at[1 - x, u], dst_ref=srecv.at[u], send_sem=xs_sem.at[u],
            recv_sem=xr_sem.at[u], device_id=(2 * i + 1 - x, hd), device_id_type=MESH)

    for h in range(hh):
        loads[h][0].wait()
        loads[h][1].wait()
        mst[h] = jnp.zeros((dqk, dv), BF16)
        norm8[h:h + 1, :] = jnp.zeros((1, dqk), F32)
        for j in range(nh):
            r = j * hh + h
            kt = k_v[h, j * L:(j + 1) * L, :].T.astype(F32)
            kw = kt * w3[r]
            part = kw[:, 0:128]
            for b in range(1, L // 128):
                part = part + kw[:, b * 128:(b + 1) * 128]
            nrow = jnp.sum(part.T, axis=0, keepdims=True)
            upd = jnp.dot(kw.astype(BF16), v_v[h, j * L:(j + 1) * L, :], preferred_element_type=F32)
            if j > 0:
                kp = keep[j][h:h + 1, 0:1]
                upd = upd + kp * st[...]
                nrow = nrow + kp * norm_st[...]
            if j < nh - 1:
                st[...] = upd
                norm_st[...] = nrow
                mst[(j + 1) * hh + h] = upd.astype(BF16)
                norm8[(j + 1) * hh + h:(j + 1) * hh + h + 1, :] = nrow
            else:
                for cc in range(cph):
                    for b in range(pairs):
                        for xx in range(2):
                            r0 = (2 * b + xx) * R
                            sbuf[xx, h * cph + cc, b * R:(b + 1) * R, :] = upd[
                                r0:r0 + R, cc * CW:(cc + 1) * CW]
                    s_copy(h * cph + cc).start()
                summ[c, h:h + 1, :] = nrow
    wide = jnp.ones((1, dqk), F32)
    summ[c, hh:2 * hh, :] = cg[:, 0:1] * wide
    summ[c, 2 * hh:3 * hh, :] = sl[:, 0:1] * wide

    def sum_copy(d, slot):
        return pltpu.make_async_remote_copy(
            src_ref=summ.at[slot], dst_ref=summ.at[slot], send_sem=ss_sem.at[d],
            recv_sem=sr_sem.at[d], device_id=(lax.rem(c + d, nc), hd), device_id_type=MESH)

    for d in range(1, nc):
        sum_copy(d, c).start()

    @pl.when(i == 0)
    def _():
        erecv[...] = jnp.zeros(erecv.shape, F32)

    @pl.when(c == 0)
    def _():
        xrecv[...] = jnp.zeros(xrecv.shape, F32)

    for d in range(1, nc):
        sum_copy(d, lax.rem(c + nc - d, nc)).wait_recv()

    stab = jnp.full((hh, dqk), NEG, F32)
    norm = jnp.zeros((hh, dqk), F32)
    zero = jnp.zeros((hh, dqk), F32)
    in_stab, in_norm = zero, zero
    fa = [zero, zero, zero, zero]
    for s in range(nc):
        total = summ[s, hh:2 * hh, :]
        late = summ[s, 2 * hh:3 * hh, :]
        in_stab = jnp.where(c == s, stab, in_stab)
        in_norm = jnp.where(c == s, norm, in_norm)
        new = jnp.maximum(stab + total, late)
        fe = jnp.exp(stab + total - new)
        fl = jnp.exp(late - new)
        o = 2 * (s % 2)
        fa[o] = jnp.where(i == s // 2, fe, fa[o])
        fa[o + 1] = jnp.where(i == s // 2, fl, fa[o + 1])
        norm = fe * norm + fl * summ[s, 0:hh, :]
        stab = new
    norm_out[...] = norm
    max_out[...] = stab[:, 0:128]
    for h in range(hh):
        for o in range(4):
            fac[h, o:o + 1, :] = fa[o][h:h + 1, 0:128]
    insr8 = jnp.concatenate([in_stab[:, 0:128]] * nh, axis=0) + cg8
    sg8 = jnp.maximum(slp8, insr8)
    m = jnp.maximum(amax_run, sg8[:, 0:1])
    ng = (jnp.exp(slp8 - sg8)[:, 0:1] * norm8[...]
          + jnp.exp(insr8 - sg8)[:, 0:1] * jnp.concatenate([in_norm] * nh, axis=0))
    mt = m.T
    for r in range(nt):
        insr3[r] = insr8[r:r + 1, :]
        sg3[r] = sg8[r:r + 1, :]
        ng3[r] = ng[r:r + 1, :]
        mcolb[r] = jnp.broadcast_to(mt[:, r:r + 1], (L, 128))
    for h in range(hh):
        loads[h][2].wait()

    tt = min(256, L)

    def intra(task):
        h = task // nh
        j = task - h * nh
        r = j * hh + h
        base = pl.multiple_of(j * L, L)
        for rt in range(L // tt):
            t0 = rt * tt
            ncol = t0 + tt
            rows = pl.ds(pl.multiple_of(base + t0, tt), tt)
            q = q_v[h, rows, :]
            mc = mcolb[r, t0:t0 + tt, :]
            kk = k_v[h, pl.ds(base, ncol), :]
            vv = v_v[h, pl.ds(base, ncol), :]
            s = lax.dot_general(q, kk, (((1,), (1,)), ((), ())), preferred_element_type=F32)
            e = jnp.exp(a3[r][:, 0:ncol] - mc[:, 0:1])
            ti = lax.broadcasted_iota(jnp.int32, (tt, ncol), 0) + t0
            si = lax.broadcasted_iota(jnp.int32, (tt, ncol), 1)
            mixed = jnp.where(ti >= si, e, 0.0) * (s * scale)
            qn = jnp.sum(q.astype(F32) * ng3[r], axis=1, keepdims=True)
            den = jnp.sum(mixed, axis=1, keepdims=True) + jnp.exp(sg3[r] - mc)[:, 0:1] * qn
            inv = 1.0 / jnp.maximum(jnp.abs(den), 1.0)
            num = jnp.dot(mixed.astype(BF16), vv, preferred_element_type=F32)
            loc = jnp.dot(q, mst[r], preferred_element_type=F32)
            num = num * inv + (jnp.exp(slp3[r] - mc)[:, 0:1] * inv) * loc
            for cc in range(cph):
                numn[h * cph + cc, rows, :] = num[:, cc * CW:(cc + 1) * CW]
            cinb[h, rows, :] = jnp.exp(insr3[r] - mc) * inv

    def e_copy(u):
        to = lax.rem(c + 2, nc)
        return pltpu.make_async_remote_copy(
            src_ref=eout.at[u], dst_ref=erecv.at[u], send_sem=es_sem.at[u],
            recv_sem=er_sem.at[u], device_id=(to, hd), device_id_type=MESH)

    def f_copy(u):
        return pltpu.make_async_remote_copy(
            src_ref=xsend.at[u], dst_ref=xrecv.at[u], send_sem=fs_sem.at[u],
            recv_sem=fr_sem.at[u], device_id=(2 * i + 1 - x, hd), device_id_type=MESH)

    def c_copy(u, b):
        return pltpu.make_async_remote_copy(
            src_ref=eout.at[u, pl.ds(b * R, R), :], dst_ref=closb.at[u],
            send_sem=cs_sem.at[u, b], recv_sem=cr_sem.at[u],
            device_id=(2 * b + x, hd), device_id_type=MESH)

    per = nt // nu

    def step(u, carry):
        for o in range(per):
            intra(u * per + o)
        h = u // cph
        s_copy(u).wait_recv()

        @pl.when(i > 0)
        def _():
            e_copy(u).wait_recv()

        mine = sbuf[x, u]
        other = srecv[u]
        e = erecv[u]
        f = fac[h]
        first = jnp.where(x == 0, mine, other)
        second = jnp.where(x == 0, other, mine)
        mid = f[0:1, :] * e + f[1:2, :] * first
        eout[u] = f[2:3, :] * mid + f[3:4, :] * second
        xsend[u] = jnp.where(x == 0, mid, e)
        own[u] = jnp.where(x == 0, e, mid)

        @pl.when(i < pairs - 1)
        def _():
            e_copy(u).start()

        @pl.when(c != 1)
        def _():
            f_copy(u).start()

        @pl.when(i == pairs - 1)
        def _():
            for b in range(pairs - 1):
                c_copy(u, b).start()
            closb[u] = eout[u, (pairs - 1) * R:pairs * R, :]

        return carry

    lax.fori_loop(0, nu, step, 0)

    rt = min(512, toks)

    def out_copy(u):
        return pltpu.make_async_copy(
            outb.at[u], out_hbm.at[:, pl.ds(pl.multiple_of(u * CW, CW), CW)], out_sem.at[u])

    def final(u, carry):
        h = u // cph

        @pl.when(c > 0)
        def _():
            f_copy(u).wait_recv()

        inm[:, x] = own[u].reshape(pairs, R, CW)
        inm[:, 1 - x] = xrecv[u].reshape(pairs, R, CW)
        mem = inm[...].reshape(dqk, CW).astype(BF16)
        for b in range(toks // rt):
            rows = pl.ds(b * rt, rt)
            got = jnp.dot(q_v[h, rows, :], mem, preferred_element_type=F32)
            outb[u, rows, :] = (numn[u, rows, :] + cinb[h, rows, :] * got).astype(BF16)
        out_copy(u).start()
        return carry

    lax.fori_loop(0, nu, final, 0)

    for u in range(nu):
        @pl.when(i < pairs - 1)
        def _():
            c_copy(u, i).wait_recv()

        h, cc = u // cph, u % cph
        clos_out[h, :, cc * CW:(cc + 1) * CW] = closb[u]

    for d in range(1, nh):
        gate_copy(d).wait_send()
    for d in range(1, nc):
        sum_copy(d, c).wait_send()

    def drain(u, carry):
        s_copy(u).wait_send()

        @pl.when(i < pairs - 1)
        def _():
            e_copy(u).wait_send()

        @pl.when(c != 1)
        def _():
            f_copy(u).wait_send()

        @pl.when(i == pairs - 1)
        def _():
            for b in range(pairs - 1):
                c_copy(u, b).wait_send()

        out_copy(u).wait()
        return carry

    lax.fori_loop(0, nu, drain, 0)


def on_device(nc, nh, queries, keys, values, gate_pre):
    toks = queries.shape[0]
    hh = gate_pre.shape[1] // nh
    dqk = queries.shape[1] // hh
    dv = values.shape[1] // hh
    L = toks // nh
    R = dqk // nc
    pairs = nc // 2
    nu = hh * dv // CW
    nt = hh * nh
    half = dqk // 2
    vm = pltpu.VMEM
    dma = pltpu.SemaphoreType.DMA
    anyspec = pl.BlockSpec(memory_space=pl.ANY)
    vspec = pl.BlockSpec(memory_space=pltpu.VMEM)
    macs = hh * toks * (L * (dqk + dv) + 3 * dqk * dv)
    hidden, closing, norm, top = pl.pallas_call(
        functools.partial(kernel, nc, nh, hh, toks, dqk, dv),
        out_shape=(
            jax.ShapeDtypeStruct((toks, hh * dv), BF16),
            jax.ShapeDtypeStruct((hh, R, dv), F32),
            jax.ShapeDtypeStruct((hh, dqk), F32),
            jax.ShapeDtypeStruct((hh, 128), F32),
        ),
        in_specs=[anyspec] * 4,
        out_specs=(anyspec, vspec, vspec, vspec),
        scratch_shapes=[
            vm((hh, toks, dqk), BF16), vm((hh, toks, dqk), BF16), vm((hh, toks, dv), BF16),
            vm(gate_pre.shape, F32), vm((nh, 8, L), F32), vm((nh, 8, L), F32),
            vm((nt, L), F32), vm((nt, L), F32),
            vm((nt, 1, L), F32), vm((nt, L, 128), F32), vm((nt, 1, L), F32),
            vm((nt, 1, 128), F32), vm((nt, 1, 128), F32), vm((nt, 1, 128), F32),
            vm((nt, 1, dqk), F32), vm((nt, dqk), F32), vm((nt, dqk, dv), BF16),
            vm((dqk, dv), F32), vm((1, dqk), F32),
            vm((nc, 8, dqk), F32), vm((hh, 8, 128), F32),
            vm((2, nu, half, CW), F32), vm((nu, half, CW), F32), vm((nu, half, CW), F32),
            vm((nu, half, CW), F32), vm((nu, half, CW), F32), vm((nu, half, CW), F32),
            vm((nu, half, CW), F32), vm((nu, R, CW), F32), vm((pairs, 2, R, CW), F32),
            vm((nu, toks, CW), F32), vm((hh, toks, 128), F32), vm((nu, toks, CW), BF16),
            dma((1 + 3 * hh,)), dma((nh,)), dma((nh,)), dma((nc,)), dma((nc,)),
            dma((nu,)), dma((nu,)), dma((nu,)), dma((nu,)), dma((nu,)), dma((nu,)),
            dma((nu, pairs)), dma((nu,)), dma((nu,)),
        ],
        compiler_params=pltpu.CompilerParams(
            collective_id=0, has_side_effects=True, vmem_limit_bytes=56 * 1024 * 1024),
        cost_estimate=pl.CostEstimate(
            flops=2 * macs, bytes_accessed=12 * 1024 * 1024, transcendentals=hh * toks * L),
        name="mlstm",
    )(queries, keys, values, gate_pre)
    return hidden, closing, norm, top[:, 0]


def solution(mesh):
    nc, nh = mesh.shape["ctx"], mesh.shape["head"]
    in_specs = (
        P("ctx", "head"),
        P("ctx", "head"),
        P("ctx", "head"),
        P(None, None, ("ctx", "head")),
    )
    out_specs = (P("ctx", "head"), P("head", "ctx", None), P("head", None), P("head"))
    return jax.shard_map(
        functools.partial(on_device, nc, nh),
        mesh=mesh, in_specs=in_specs, out_specs=out_specs, check_vma=False,
    )
```

time: 308 us -> 60.4 us (0.20)
  blocking collectives: 86.7 us -> 0 us
  waiting for transfers between devices: 65 us -> 0 us
  matrix products: 57.7 us -> 0 us
  local copies, waits for them, and re-layouts: 61.8 us -> 7.2 us
  Pallas kernels: 0 us -> 52.4 us
  other arithmetic: 14.6 us -> 0 us
  between operations: 14.9 us -> 0.64 us
  starting transfers between devices: 4.28 us -> 0 us
    dot_general x22 -> x0, matrix products: 57.7 us -> none  [the longest x4 14.1 us: block_step(): jnp.dot(q_float, memory, precision=lax.Precision.HIGHEST)]
    pallas_call x0 -> x1, Pallas kernels: none -> 52.4 us  [on_device(): pl.pallas_call(functools.partial(kernel, nc, nh, hh, toks, dqk, dv), out_...]
    reduce_scatter x1 -> x0, waiting for transfers between devices: 48.3 us -> none  [on_device(): lax.psum_scatter(memory * factor[:, None, None], 'ctx', scatter_dimension...]
    unnamed x2 -> x0, blocking collectives: 42.3 us -> none
    all_gather x1 -> x0, blocking collectives: 26.5 us -> none  [prefix(): gathered = jax.tree.map(lambda a: lax.all_gather(a, axis), part)]
    transpose x5 -> x0, local copies, waits for them, and re-layouts: 23.4 us -> none  [the longest x1 10.4 us: local_chain(): numer.reshape(row_entries, width)]
    unnamed x20 -> x7, local copies, waits for them, and re-layouts: 25.5 us -> 5.92 us
    pmax x1 -> x0, blocking collectives: 17.8 us -> none  [on_device(): final_max = lax.pmax(at_end, 'ctx')]
  transfers between devices with their start and end apart: 3 -> 0, of which waited for: 2 -> 0; matrix products, arithmetic and copies ran while one was open for 22% -> 0% of each run, Pallas kernels for 0% -> 0%
where the time goes in v1:
time: 60.4 us; the launch traced here: 60.3 us
  Pallas kernels  52.4 us (87%)
  local copies, waits for them, and re-layouts  7.2 us (12%)
  between operations  0.64 us (1%)
    pallas_call x1, Pallas kernels, on_device(): pl.pallas_call(functools.partial(kernel, nc, nh, hh, toks, dqk, dv), out_...  52.4 us
    unnamed x7, local copies, waits for them, and re-layouts  5.92 us
    slice x1, local copies, waits for them, and re-layouts, on_device(): return (hidden, closing, norm, top[:, 0])  1.29 us

profile of v1, /device:TPU:0, one launch (start us, length us, event | category | flops | bytes accessed | tf_op | source)
XLA Modules:
  0.0 60.3 jit_solution(17433883047158038011)
XLA Ops:
  0.6 52.4 %mlstm.1 = (bf16[2048,1024]{1,0:T(8,128)(2,1)}, f32[2,32,512]{2,1,0:T(8,128)}, f32[2,256]{1,0:T(2,128)}, f32[2,128]{1,0:T(2,128)}) custom-call(bf16[2048,512]{1,0:T(8,128)(2,1)} %q_hbm.1, bf16[2048,512]{1,0:T(8,128)(2,1)} %k_hbm.1, bf16[2048,1024]{1,0:T(8,128)(2,1)} %v_hbm.1, f32[2,8,512]{2,1,0:T(8,128)} %g_hbm.1), custom_call_target="tpu_custom_call" | custom-call | flops 6442450944 | bytes 12582912 | tf_op jit(solution)/shard_map/mlstm/pallas_call | solution.py:390
  53.1 1.3 %slice_reduce_fusion = f32[2]{0:T(128)} fusion(f32[2,128]{1,0:T(2,128)} %get-tuple-element.11), kind=kLoop, calls=%fused_computation | loop fusion | bytes 16 | tf_op jit(solution)/shard_map/slice | solution.py:423
  54.4 0.0 copy-start
  54.4 0.0 copy-start.1
  54.4 4.7 %copy.11 = bf16[2048,1024]{1,0:T(8,128)(2,1)} copy(bf16[2048,1024]{1,0:T(8,128)(2,1)} %get-tuple-element.16) | data formatting | bytes 8388608
  59.0 0.0 copy-done
  59.0 0.7 %copy.12 = f32[2,32,512]{2,1,0:T(8,128)} copy(f32[2,32,512]{2,1,0:T(8,128)S(1)} %copy-done) | data formatting | bytes 262144
  59.7 0.0 copy-done.1
  59.7 0.6 copy.13
Async XLA Ops:
  54.4 4.7 %copy-start = (f32[2,32,512]{2,1,0:T(8,128)S(1)}, f32[2,32,512]{2,1,0:T(8,128)}, u32[]{:S(2)}) copy-start(f32[2,32,512]{2,1,0:T(8,128)} %get-tuple-element.17) | copy-start | bytes 393220
  54.4 5.3 %copy-start.1 = (f32[2,256]{1,0:T(2,128)S(1)}, f32[2,256]{1,0:T(2,128)}, u32[]{:S(2)}) copy-start(f32[2,256]{1,0:T(2,128)} %get-tuple-element.18) | copy-start | bytes 6148

commit v2 on v1

--- a/solution.py
+++ b/solution.py
@@ -21,13 +21,13 @@
 def kernel(
     nc, nh, hh, toks, dqk, dv,
     q_hbm, k_hbm, v_hbm, g_hbm,
-    out_hbm, clos_out, norm_out, max_out,
-    q_v, k_v, v_v, g_v, gsend, grecv, ig_s, fg_s,
-    a3, mcolb, w3, slp3, insr3, sg3, ng3, norm8, mst, st, norm_st,
+    num_hbm, qs_hbm, mem_out, clos_out, norm_out, max_out,
+    q_v, k_v, v_v, g_v, gsend, grecv, ig_s, fg_s, kt_v, kw_v,
+    a3, mcolb, w3, slp3, insr3, sg3, ng3, norm8, mst, st,
     summ, fac, sbuf, srecv, erecv, eout, xsend, xrecv, own, closb, inm,
-    numn, cinb, outb,
+    numv, qsv,
     in_sem, gs_sem, gr_sem, ss_sem, sr_sem, xs_sem, xr_sem,
-    es_sem, er_sem, fs_sem, fr_sem, cs_sem, cr_sem, out_sem,
+    es_sem, er_sem, fs_sem, fr_sem, cs_sem, cr_sem, num_sem, qs_sem,
 ):
     c = lax.axis_index("ctx")
     hd = lax.axis_index("head")
@@ -84,6 +84,10 @@
     for d in range(1, nh):
         gate_copy(d).start()
     grecv[hd] = gsend[hd]
+    for h in range(hh):
+        loads[h][0].wait()
+        for j in range(nh):
+            kt_v[j * hh + h] = k_v[h, j * L:(j + 1) * L, :].T
     for d in range(1, nh):
         gate_wait(d).wait_recv()
     for p in range(nh):
@@ -99,13 +103,8 @@
         cum = cum + shifted(cum, k, lane, 0.0)
         k *= 2
     a = ig - cum
-    amax_run = a
-    k = 1
-    while k < L:
-        amax_run = jnp.maximum(amax_run, shifted(amax_run, k, lane, NEG))
-        k *= 2
     gb = jnp.broadcast_to(cum[:, L - 1:L], (nt, 128))
-    ab = jnp.broadcast_to(amax_run[:, L - 1:L], (nt, 128))
+    ab = jnp.broadcast_to(jnp.max(a, axis=1, keepdims=True), (nt, 128))
     sl = jnp.full((hh, 128), NEG, F32)
     cg = jnp.zeros((hh, 128), F32)
     before, after, gone, keep = [], [], [], []
@@ -131,29 +130,44 @@
             src_ref=sbuf.at[1 - x, u], dst_ref=srecv.at[u], send_sem=xs_sem.at[u],
             recv_sem=xr_sem.at[u], device_id=(2 * i + 1 - x, hd), device_id_type=MESH)
 
-    for h in range(hh):
-        loads[h][0].wait()
-        loads[h][1].wait()
-        mst[h] = jnp.zeros((dqk, dv), BF16)
+    def sum_copy(d, slot):
+        return pltpu.make_async_remote_copy(
+            src_ref=summ.at[slot], dst_ref=summ.at[slot], send_sem=ss_sem.at[d],
+            recv_sem=sr_sem.at[d], device_id=(lax.rem(c + d, nc), hd), device_id_type=MESH)
+
+    for h in range(hh):
         norm8[h:h + 1, :] = jnp.zeros((1, dqk), F32)
+        run = None
         for j in range(nh):
             r = j * hh + h
-            kt = k_v[h, j * L:(j + 1) * L, :].T.astype(F32)
-            kw = kt * w3[r]
+            kw = kt_v[r].astype(F32) * w3[r]
             part = kw[:, 0:128]
             for b in range(1, L // 128):
                 part = part + kw[:, b * 128:(b + 1) * 128]
             nrow = jnp.sum(part.T, axis=0, keepdims=True)
-            upd = jnp.dot(kw.astype(BF16), v_v[h, j * L:(j + 1) * L, :], preferred_element_type=F32)
+            kw_v[r] = kw.astype(BF16)
+            run = nrow if j == 0 else nrow + keep[j][h:h + 1, 0:1] * run
+            if j < nh - 1:
+                norm8[r + hh:r + hh + 1, :] = run
+            else:
+                summ[c, h:h + 1, :] = run
+    wide = jnp.ones((1, dqk), F32)
+    summ[c, hh:2 * hh, :] = cg[:, 0:1] * wide
+    summ[c, 2 * hh:3 * hh, :] = sl[:, 0:1] * wide
+    for d in range(1, nc):
+        sum_copy(d, c).start()
+
+    for h in range(hh):
+        loads[h][1].wait()
+        mst[h] = jnp.zeros((dqk, dv), BF16)
+        for j in range(nh):
+            r = j * hh + h
+            upd = jnp.dot(kw_v[r], v_v[h, j * L:(j + 1) * L, :], preferred_element_type=F32)
             if j > 0:
-                kp = keep[j][h:h + 1, 0:1]
-                upd = upd + kp * st[...]
-                nrow = nrow + kp * norm_st[...]
+                upd = upd + keep[j][h:h + 1, 0:1] * st[...]
             if j < nh - 1:
                 st[...] = upd
-                norm_st[...] = nrow
-                mst[(j + 1) * hh + h] = upd.astype(BF16)
-                norm8[(j + 1) * hh + h:(j + 1) * hh + h + 1, :] = nrow
+                mst[r + hh] = upd.astype(BF16)
             else:
                 for cc in range(cph):
                     for b in range(pairs):
@@ -162,18 +176,12 @@
                             sbuf[xx, h * cph + cc, b * R:(b + 1) * R, :] = upd[
                                 r0:r0 + R, cc * CW:(cc + 1) * CW]
                     s_copy(h * cph + cc).start()
-                summ[c, h:h + 1, :] = nrow
-    wide = jnp.ones((1, dqk), F32)
-    summ[c, hh:2 * hh, :] = cg[:, 0:1] * wide
-    summ[c, 2 * hh:3 * hh, :] = sl[:, 0:1] * wide
-
-    def sum_copy(d, slot):
-        return pltpu.make_async_remote_copy(
-            src_ref=summ.at[slot], dst_ref=summ.at[slot], send_sem=ss_sem.at[d],
-            recv_sem=sr_sem.at[d], device_id=(lax.rem(c + d, nc), hd), device_id_type=MESH)
-
-    for d in range(1, nc):
-        sum_copy(d, c).start()
+
+    amax_run = a
+    k = 1
+    while k < L:
+        amax_run = jnp.maximum(amax_run, shifted(amax_run, k, lane, NEG))
+        k *= 2
 
     @pl.when(i == 0)
     def _():
@@ -225,7 +233,19 @@
 
     tt = min(256, L)
 
-    def intra(task):
+    def num_copy(task):
+        h = task // nh
+        rows = pl.ds(pl.multiple_of((task - h * nh) * L, L), L)
+        return pltpu.make_async_copy(
+            numv.at[h, rows, :], num_hbm.at[h, rows, :], num_sem.at[task])
+
+    def qs_copy(task):
+        h = task // nh
+        rows = pl.ds(pl.multiple_of((task - h * nh) * L, L), L)
+        return pltpu.make_async_copy(
+            qsv.at[h, rows, :], qs_hbm.at[h, rows, :], qs_sem.at[task])
+
+    def intra(task, carry):
         h = task // nh
         j = task - h * nh
         r = j * hh + h
@@ -236,22 +256,25 @@
             rows = pl.ds(pl.multiple_of(base + t0, tt), tt)
             q = q_v[h, rows, :]
             mc = mcolb[r, t0:t0 + tt, :]
-            kk = k_v[h, pl.ds(base, ncol), :]
+            kk = kt_v[r, :, 0:ncol]
             vv = v_v[h, pl.ds(base, ncol), :]
-            s = lax.dot_general(q, kk, (((1,), (1,)), ((), ())), preferred_element_type=F32)
+            s = jnp.dot(q, kk, preferred_element_type=F32)
             e = jnp.exp(a3[r][:, 0:ncol] - mc[:, 0:1])
             ti = lax.broadcasted_iota(jnp.int32, (tt, ncol), 0) + t0
             si = lax.broadcasted_iota(jnp.int32, (tt, ncol), 1)
             mixed = jnp.where(ti >= si, e, 0.0) * (s * scale)
-            qn = jnp.sum(q.astype(F32) * ng3[r], axis=1, keepdims=True)
+            qf = q.astype(F32)
+            qn = jnp.sum(qf * ng3[r], axis=1, keepdims=True)
             den = jnp.sum(mixed, axis=1, keepdims=True) + jnp.exp(sg3[r] - mc)[:, 0:1] * qn
             inv = 1.0 / jnp.maximum(jnp.abs(den), 1.0)
             num = jnp.dot(mixed.astype(BF16), vv, preferred_element_type=F32)
             loc = jnp.dot(q, mst[r], preferred_element_type=F32)
             num = num * inv + (jnp.exp(slp3[r] - mc)[:, 0:1] * inv) * loc
-            for cc in range(cph):
-                numn[h * cph + cc, rows, :] = num[:, cc * CW:(cc + 1) * CW]
-            cinb[h, rows, :] = jnp.exp(insr3[r] - mc) * inv
+            numv[h, rows, :] = num.astype(BF16)
+            qsv[h, rows, :] = (qf * (jnp.exp(insr3[r] - mc)[:, 0:1] * inv)).astype(BF16)
+        num_copy(task).start()
+        qs_copy(task).start()
+        return carry
 
     def e_copy(u):
         to = lax.rem(c + 2, nc)
@@ -270,11 +293,13 @@
             send_sem=cs_sem.at[u, b], recv_sem=cr_sem.at[u],
             device_id=(2 * b + x, hd), device_id_type=MESH)
 
-    per = nt // nu
+    lead = jnp.minimum(i, nt // 2)
+
+    def done(u):
+        return jnp.minimum(lead + (u + 1) // 2, nt)
 
     def step(u, carry):
-        for o in range(per):
-            intra(u * per + o)
+        lax.fori_loop(jnp.where(u == 0, 0, done(u - 1)), done(u), intra, 0)
         h = u // cph
         s_copy(u).wait_recv()
 
@@ -311,30 +336,19 @@
 
     lax.fori_loop(0, nu, step, 0)
 
-    rt = min(512, toks)
-
-    def out_copy(u):
-        return pltpu.make_async_copy(
-            outb.at[u], out_hbm.at[:, pl.ds(pl.multiple_of(u * CW, CW), CW)], out_sem.at[u])
-
-    def final(u, carry):
-        h = u // cph
-
+    lax.fori_loop(done(nu - 1), nt, intra, 0)
+
+    def gather(u, carry):
         @pl.when(c > 0)
         def _():
             f_copy(u).wait_recv()
 
         inm[:, x] = own[u].reshape(pairs, R, CW)
         inm[:, 1 - x] = xrecv[u].reshape(pairs, R, CW)
-        mem = inm[...].reshape(dqk, CW).astype(BF16)
-        for b in range(toks // rt):
-            rows = pl.ds(b * rt, rt)
-            got = jnp.dot(q_v[h, rows, :], mem, preferred_element_type=F32)
-            outb[u, rows, :] = (numn[u, rows, :] + cinb[h, rows, :] * got).astype(BF16)
-        out_copy(u).start()
+        mem_out[u] = inm[...].reshape(dqk, CW).astype(BF16)
         return carry
 
-    lax.fori_loop(0, nu, final, 0)
+    lax.fori_loop(0, nu, gather, 0)
 
     for u in range(nu):
         @pl.when(i < pairs - 1)
@@ -365,10 +379,32 @@
             for b in range(pairs - 1):
                 c_copy(u, b).wait_send()
 
-        out_copy(u).wait()
         return carry
 
     lax.fori_loop(0, nu, drain, 0)
+
+    def drain_own(task, carry):
+        num_copy(task).wait()
+        qs_copy(task).wait()
+        return carry
+
+    lax.fori_loop(0, nt, drain_own, 0)
+
+
+def readout(hh, cph, num_ref, qs_ref, mem_ref, clos_in, norm_in, max_in,
+            out_ref, clos_out, norm_out, max_out):
+    dv = cph * CW
+    for h in range(hh):
+        mem = jnp.concatenate([mem_ref[h * cph + cc] for cc in range(cph)], axis=1)
+        got = jnp.dot(qs_ref[h], mem, preferred_element_type=F32)
+        out_ref[:, h * dv:(h + 1) * dv] = (num_ref[h].astype(F32) + got).astype(BF16)
+
+    @pl.when(pl.program_id(0) == 0)
+    def _():
+        clos_out[...] = clos_in[...]
+        norm_out[...] = norm_in[...]
+        for h in range(hh):
+            max_out[h] = max_in[h, 0]
 
 
 def on_device(nc, nh, queries, keys, values, gate_pre):
@@ -387,32 +423,34 @@
     anyspec = pl.BlockSpec(memory_space=pl.ANY)
     vspec = pl.BlockSpec(memory_space=pltpu.VMEM)
     macs = hh * toks * (L * (dqk + dv) + 3 * dqk * dv)
-    hidden, closing, norm, top = pl.pallas_call(
+    num, qs, mem, closing, norm, top = pl.pallas_call(
         functools.partial(kernel, nc, nh, hh, toks, dqk, dv),
         out_shape=(
-            jax.ShapeDtypeStruct((toks, hh * dv), BF16),
+            jax.ShapeDtypeStruct((hh, toks, dv), BF16),
+            jax.ShapeDtypeStruct((hh, toks, dqk), BF16),
+            jax.ShapeDtypeStruct((nu, dqk, CW), BF16),
             jax.ShapeDtypeStruct((hh, R, dv), F32),
             jax.ShapeDtypeStruct((hh, dqk), F32),
             jax.ShapeDtypeStruct((hh, 128), F32),
         ),
         in_specs=[anyspec] * 4,
-        out_specs=(anyspec, vspec, vspec, vspec),
+        out_specs=(anyspec, anyspec, vspec, vspec, vspec, vspec),
         scratch_shapes=[
             vm((hh, toks, dqk), BF16), vm((hh, toks, dqk), BF16), vm((hh, toks, dv), BF16),
             vm(gate_pre.shape, F32), vm((nh, 8, L), F32), vm((nh, 8, L), F32),
-            vm((nt, L), F32), vm((nt, L), F32),
+            vm((nt, L), F32), vm((nt, L), F32), vm((nt, dqk, L), BF16), vm((nt, dqk, L), BF16),
             vm((nt, 1, L), F32), vm((nt, L, 128), F32), vm((nt, 1, L), F32),
             vm((nt, 1, 128), F32), vm((nt, 1, 128), F32), vm((nt, 1, 128), F32),
             vm((nt, 1, dqk), F32), vm((nt, dqk), F32), vm((nt, dqk, dv), BF16),
-            vm((dqk, dv), F32), vm((1, dqk), F32),
+            vm((dqk, dv), F32),
             vm((nc, 8, dqk), F32), vm((hh, 8, 128), F32),
             vm((2, nu, half, CW), F32), vm((nu, half, CW), F32), vm((nu, half, CW), F32),
             vm((nu, half, CW), F32), vm((nu, half, CW), F32), vm((nu, half, CW), F32),
             vm((nu, half, CW), F32), vm((nu, R, CW), F32), vm((pairs, 2, R, CW), F32),
-            vm((nu, toks, CW), F32), vm((hh, toks, 128), F32), vm((nu, toks, CW), BF16),
+            vm((hh, toks, dv), BF16), vm((hh, toks, dqk), BF16),
             dma((1 + 3 * hh,)), dma((nh,)), dma((nh,)), dma((nc,)), dma((nc,)),
             dma((nu,)), dma((nu,)), dma((nu,)), dma((nu,)), dma((nu,)), dma((nu,)),
-            dma((nu, pairs)), dma((nu,)), dma((nu,)),
+            dma((nu, pairs)), dma((nu,)), dma((nt,)), dma((nt,)),
         ],
         compiler_params=pltpu.CompilerParams(
             collective_id=0, has_side_effects=True, vmem_limit_bytes=56 * 1024 * 1024),
@@ -420,7 +458,30 @@
             flops=2 * macs, bytes_accessed=12 * 1024 * 1024, transcendentals=hh * toks * L),
         name="mlstm",
     )(queries, keys, values, gate_pre)
-    return hidden, closing, norm, top[:, 0]
+    tb = min(256, toks)
+    return pl.pallas_call(
+        functools.partial(readout, hh, dv // CW),
+        grid=(toks // tb,),
+        out_shape=(
+            jax.ShapeDtypeStruct((toks, hh * dv), BF16),
+            jax.ShapeDtypeStruct((hh, R, dv), F32),
+            jax.ShapeDtypeStruct((hh, dqk), F32),
+            jax.ShapeDtypeStruct((hh,), F32),
+        ),
+        in_specs=[
+            pl.BlockSpec((hh, tb, dv), lambda t: (0, t, 0)),
+            pl.BlockSpec((hh, tb, dqk), lambda t: (0, t, 0)),
+            vspec, vspec, vspec, pl.BlockSpec(memory_space=pltpu.SMEM),
+        ],
+        out_specs=(
+            pl.BlockSpec((tb, hh * dv), lambda t: (t, 0)),
+            vspec, vspec, pl.BlockSpec(memory_space=pltpu.SMEM),
+        ),
+        compiler_params=pltpu.CompilerParams(vmem_limit_bytes=60 * 1024 * 1024),
+        cost_estimate=pl.CostEstimate(
+            flops=2 * hh * toks * dqk * dv, bytes_accessed=11 * 1024 * 1024, transcendentals=0),
+        name="readout",
+    )(num, qs, mem, closing, norm, top)
 
 
 def solution(mesh):

time: 60.4 us -> 50.1 us (0.83)
  local copies, waits for them, and re-layouts: 7.2 us -> 0 us
  Pallas kernels: 52.4 us -> 49.2 us
    pallas_call x1, Pallas kernels: 52.4 us -> 40.9 us  [on_device(): pl.pallas_call(functools.partial(kernel, nc, nh, hh, toks, dqk, dv), out_...]
    pallas_call x0 -> x1, Pallas kernels: none -> 8.27 us  [on_device(): pl.pallas_call(functools.partial(readout, hh, dv // CW), grid=(toks // tb...]
    unnamed x7 -> x0, local copies, waits for them, and re-layouts: 5.92 us -> none
    slice x1 -> x0, local copies, waits for them, and re-layouts: 1.29 us -> none  [on_device(): return (hidden, closing, norm, top[:, 0])]
where the time goes in v2:
time: 50.1 us; the launch traced here: 49.8 us
  Pallas kernels  49.2 us (98%)
  between operations  0.64 us (1%)
    pallas_call x1, Pallas kernels, on_device(): pl.pallas_call(functools.partial(kernel, nc, nh, hh, toks, dqk, dv), out_...  40.9 us
    pallas_call x1, Pallas kernels, on_device(): pl.pallas_call(functools.partial(readout, hh, dv // CW), grid=(toks // tb...  8.27 us

profile of v2, /device:TPU:0, one launch (start us, length us, event | category | flops | bytes accessed | tf_op | source)
XLA Modules:
  0.0 49.8 jit_solution(15706608541384570141)
XLA Ops:
  0.6 40.9 %mlstm.1 = (bf16[2,2048,512]{2,1,0:T(8,128)(2,1)}, bf16[2,2048,256]{2,1,0:T(8,128)(2,1)}, bf16[8,256,128]{2,1,0:T(8,128)(2,1)}, f32[2,32,512]{2,1,0:T(8,128)}, f32[2,256]{1,0:T(2,128)}, /*index=5*/f32[2,128]{1,0:T(2,128)}) custom-call(bf16[2048,512]{1,0:T(8,128)(2,1)} %q_hbm.1, bf16[2048,512]{1,0:T(8,128)(2,1)} %k_hbm.1, bf16[2048,1024]{1,0:T(8,128)(2,1)} %v_hbm.1, ...), custom_call_target="tpu_custom_call" | custom-call | flops 6442450944 | bytes 12582912 | tf_op jit(solution)/shard_map/mlstm/pallas_call | solution.py:426
  41.5 8.3 %readout.1 = (bf16[2048,1024]{1,0:T(8,128)(2,1)}, f32[2,32,512]{2,1,0:T(8,128)}, f32[2,256]{1,0:T(2,128)}, f32[2]{0:T(128)}) custom-call(bf16[2,2048,512]{2,1,0:T(8,128)(2,1)} %get-tuple-element.10.num_ref, bf16[2,2048,256]{2,1,0:T(8,128)(2,1)} %get-tuple-element.11.qs_ref, bf16[8,256,128]{2,1,0:T(8,128)(2,1)} %get-tuple-element.12.mem_ref, ...), custom_call_target="tpu_custom_call" | custom-call | flops 1073741824 | bytes 11534336 | tf_op jit(solution)/shard_map/readout/pallas_call | solution.py:462

commit v3 on v2

--- a/solution.py
+++ b/solution.py
@@ -21,13 +21,12 @@
 def kernel(
     nc, nh, hh, toks, dqk, dv,
     q_hbm, k_hbm, v_hbm, g_hbm,
-    num_hbm, qs_hbm, mem_out, clos_out, norm_out, max_out,
+    numv, qsv, mem_out, clos_out, norm_out, max_out,
     q_v, k_v, v_v, g_v, gsend, grecv, ig_s, fg_s, kt_v, kw_v,
     a3, mcolb, w3, slp3, insr3, sg3, ng3, norm8, mst, st,
     summ, fac, sbuf, srecv, erecv, eout, xsend, xrecv, own, closb, inm,
-    numv, qsv,
     in_sem, gs_sem, gr_sem, ss_sem, sr_sem, xs_sem, xr_sem,
-    es_sem, er_sem, fs_sem, fr_sem, cs_sem, cr_sem, num_sem, qs_sem,
+    es_sem, er_sem, fs_sem, fr_sem, cs_sem, cr_sem,
 ):
     c = lax.axis_index("ctx")
     hd = lax.axis_index("head")
@@ -55,8 +54,6 @@
     for h in range(hh):
         loads[h][0].start()
         loads[h][1].start()
-    for h in range(hh):
-        loads[h][2].start()
 
     barrier = pltpu.get_barrier_semaphore()
     for d in range(1, nh):
@@ -87,7 +84,8 @@
     for h in range(hh):
         loads[h][0].wait()
         for j in range(nh):
-            kt_v[j * hh + h] = k_v[h, j * L:(j + 1) * L, :].T
+            kt_v[j * hh + h] = (k_v[h, j * L:(j + 1) * L, :] * jnp.asarray(scale, BF16)).T
+        loads[h][2].start()
     for d in range(1, nh):
         gate_wait(d).wait_recv()
     for p in range(nh):
@@ -119,7 +117,7 @@
         after.append(sl)
     slp8 = jnp.concatenate(before, axis=0)
     cg8 = jnp.concatenate(gone, axis=0)
-    w = jnp.exp(a + (gb - jnp.concatenate(after, axis=0))[:, 0:1]) * scale
+    w = jnp.exp(a + (gb - jnp.concatenate(after, axis=0))[:, 0:1])
     for r in range(nt):
         a3[r] = a[r:r + 1, :]
         w3[r] = w[r:r + 1, :]
@@ -233,17 +231,8 @@
 
     tt = min(256, L)
 
-    def num_copy(task):
-        h = task // nh
-        rows = pl.ds(pl.multiple_of((task - h * nh) * L, L), L)
-        return pltpu.make_async_copy(
-            numv.at[h, rows, :], num_hbm.at[h, rows, :], num_sem.at[task])
-
-    def qs_copy(task):
-        h = task // nh
-        rows = pl.ds(pl.multiple_of((task - h * nh) * L, L), L)
-        return pltpu.make_async_copy(
-            qsv.at[h, rows, :], qs_hbm.at[h, rows, :], qs_sem.at[task])
+    tri = (lax.broadcasted_iota(jnp.int32, (tt, 128), 0)
+           - lax.broadcasted_iota(jnp.int32, (tt, 128), 1))
 
     def intra(task, carry):
         h = task // nh
@@ -256,24 +245,34 @@
             rows = pl.ds(pl.multiple_of(base + t0, tt), tt)
             q = q_v[h, rows, :]
             mc = mcolb[r, t0:t0 + tt, :]
-            kk = kt_v[r, :, 0:ncol]
-            vv = v_v[h, pl.ds(base, ncol), :]
-            s = jnp.dot(q, kk, preferred_element_type=F32)
-            e = jnp.exp(a3[r][:, 0:ncol] - mc[:, 0:1])
-            ti = lax.broadcasted_iota(jnp.int32, (tt, ncol), 0) + t0
-            si = lax.broadcasted_iota(jnp.int32, (tt, ncol), 1)
-            mixed = jnp.where(ti >= si, e, 0.0) * (s * scale)
+            s = jnp.dot(q, kt_v[r, :, 0:ncol], preferred_element_type=F32)
             qf = q.astype(F32)
-            qn = jnp.sum(qf * ng3[r], axis=1, keepdims=True)
-            den = jnp.sum(mixed, axis=1, keepdims=True) + jnp.exp(sg3[r] - mc)[:, 0:1] * qn
-            inv = 1.0 / jnp.maximum(jnp.abs(den), 1.0)
-            num = jnp.dot(mixed.astype(BF16), vv, preferred_element_type=F32)
+            ar, ng = a3[r], ng3[r]
+            qn = qf[:, 0:128] * ng[:, 0:128]
+            for b in range(1, dqk // 128):
+                qn = qn + qf[:, b * 128:(b + 1) * 128] * ng[:, b * 128:(b + 1) * 128]
+            den = jnp.exp(sg3[r] - mc) * qn
+            mixed = []
+            for b in range(ncol // 128):
+                e = jnp.exp(ar[:, b * 128:(b + 1) * 128] - mc)
+                if b * 128 >= t0:
+                    e = jnp.where(tri + t0 >= b * 128, e, 0.0)
+                e = e * s[:, b * 128:(b + 1) * 128]
+                den = den + e
+                mixed.append(e.astype(BF16))
+            den = jnp.sum(den, axis=1, keepdims=True)
+            inv = jnp.broadcast_to(1.0 / jnp.maximum(jnp.abs(den), 1.0), (tt, 128))
+            num = jnp.dot(jnp.concatenate(mixed, axis=1), v_v[h, pl.ds(base, ncol), :],
+                          preferred_element_type=F32)
             loc = jnp.dot(q, mst[r], preferred_element_type=F32)
-            num = num * inv + (jnp.exp(slp3[r] - mc)[:, 0:1] * inv) * loc
-            numv[h, rows, :] = num.astype(BF16)
-            qsv[h, rows, :] = (qf * (jnp.exp(insr3[r] - mc)[:, 0:1] * inv)).astype(BF16)
-        num_copy(task).start()
-        qs_copy(task).start()
+            cl = jnp.exp(slp3[r] - mc) * inv
+            ci = jnp.exp(insr3[r] - mc) * inv
+            for b in range(dv // 128):
+                cols = slice(b * 128, (b + 1) * 128)
+                numv[h, rows, cols] = (num[:, cols] * inv + cl * loc[:, cols]).astype(BF16)
+            for b in range(dqk // 128):
+                cols = slice(b * 128, (b + 1) * 128)
+                qsv[h, rows, cols] = (qf[:, cols] * ci).astype(BF16)
         return carry
 
     def e_copy(u):
@@ -383,21 +382,16 @@
 
     lax.fori_loop(0, nu, drain, 0)
 
-    def drain_own(task, carry):
-        num_copy(task).wait()
-        qs_copy(task).wait()
-        return carry
-
-    lax.fori_loop(0, nt, drain_own, 0)
-
 
 def readout(hh, cph, num_ref, qs_ref, mem_ref, clos_in, norm_in, max_in,
             out_ref, clos_out, norm_out, max_out):
     dv = cph * CW
+    tb = out_ref.shape[0]
+    rows = pl.ds(pl.multiple_of(pl.program_id(0) * tb, tb), tb)
     for h in range(hh):
         mem = jnp.concatenate([mem_ref[h * cph + cc] for cc in range(cph)], axis=1)
-        got = jnp.dot(qs_ref[h], mem, preferred_element_type=F32)
-        out_ref[:, h * dv:(h + 1) * dv] = (num_ref[h].astype(F32) + got).astype(BF16)
+        got = jnp.dot(qs_ref[h, rows, :], mem, preferred_element_type=F32)
+        out_ref[:, h * dv:(h + 1) * dv] = (num_ref[h, rows, :].astype(F32) + got).astype(BF16)
 
     @pl.when(pl.program_id(0) == 0)
     def _():
@@ -423,18 +417,20 @@
     anyspec = pl.BlockSpec(memory_space=pl.ANY)
     vspec = pl.BlockSpec(memory_space=pltpu.VMEM)
     macs = hh * toks * (L * (dqk + dv) + 3 * dqk * dv)
+    queries, keys, values, gate_pre = (
+        pltpu.with_memory_space_constraint(t, pltpu.HBM) for t in (queries, keys, values, gate_pre))
     num, qs, mem, closing, norm, top = pl.pallas_call(
         functools.partial(kernel, nc, nh, hh, toks, dqk, dv),
         out_shape=(
-            jax.ShapeDtypeStruct((hh, toks, dv), BF16),
-            jax.ShapeDtypeStruct((hh, toks, dqk), BF16),
-            jax.ShapeDtypeStruct((nu, dqk, CW), BF16),
+            vm((hh, toks, dv), BF16),
+            vm((hh, toks, dqk), BF16),
+            vm((nu, dqk, CW), BF16),
             jax.ShapeDtypeStruct((hh, R, dv), F32),
             jax.ShapeDtypeStruct((hh, dqk), F32),
             jax.ShapeDtypeStruct((hh, 128), F32),
         ),
         in_specs=[anyspec] * 4,
-        out_specs=(anyspec, anyspec, vspec, vspec, vspec, vspec),
+        out_specs=(vspec,) * 6,
         scratch_shapes=[
             vm((hh, toks, dqk), BF16), vm((hh, toks, dqk), BF16), vm((hh, toks, dv), BF16),
             vm(gate_pre.shape, F32), vm((nh, 8, L), F32), vm((nh, 8, L), F32),
@@ -447,18 +443,20 @@
             vm((2, nu, half, CW), F32), vm((nu, half, CW), F32), vm((nu, half, CW), F32),
             vm((nu, half, CW), F32), vm((nu, half, CW), F32), vm((nu, half, CW), F32),
             vm((nu, half, CW), F32), vm((nu, R, CW), F32), vm((pairs, 2, R, CW), F32),
-            vm((hh, toks, dv), BF16), vm((hh, toks, dqk), BF16),
             dma((1 + 3 * hh,)), dma((nh,)), dma((nh,)), dma((nc,)), dma((nc,)),
             dma((nu,)), dma((nu,)), dma((nu,)), dma((nu,)), dma((nu,)), dma((nu,)),
-            dma((nu, pairs)), dma((nu,)), dma((nt,)), dma((nt,)),
+            dma((nu, pairs)), dma((nu,)),
         ],
         compiler_params=pltpu.CompilerParams(
-            collective_id=0, has_side_effects=True, vmem_limit_bytes=56 * 1024 * 1024),
+            collective_id=0, has_side_effects=True, vmem_limit_bytes=54 * 1024 * 1024),
         cost_estimate=pl.CostEstimate(
             flops=2 * macs, bytes_accessed=12 * 1024 * 1024, transcendentals=hh * toks * L),
         name="mlstm",
     )(queries, keys, values, gate_pre)
     tb = min(256, toks)
+    num = pltpu.with_memory_space_constraint(num, pltpu.VMEM)
+    qs = pltpu.with_memory_space_constraint(qs, pltpu.VMEM)
+    mem = pltpu.with_memory_space_constraint(mem, pltpu.VMEM)
     return pl.pallas_call(
         functools.partial(readout, hh, dv // CW),
         grid=(toks // tb,),
@@ -469,15 +467,13 @@
             jax.ShapeDtypeStruct((hh,), F32),
         ),
         in_specs=[
-            pl.BlockSpec((hh, tb, dv), lambda t: (0, t, 0)),
-            pl.BlockSpec((hh, tb, dqk), lambda t: (0, t, 0)),
-            vspec, vspec, vspec, pl.BlockSpec(memory_space=pltpu.SMEM),
+            vspec, vspec, vspec, vspec, vspec, pl.BlockSpec(memory_space=pltpu.SMEM),
         ],
         out_specs=(
             pl.BlockSpec((tb, hh * dv), lambda t: (t, 0)),
             vspec, vspec, pl.BlockSpec(memory_space=pltpu.SMEM),
         ),
-        compiler_params=pltpu.CompilerParams(vmem_limit_bytes=60 * 1024 * 1024),
+        compiler_params=pltpu.CompilerParams(vmem_limit_bytes=16 * 1024 * 1024),
         cost_estimate=pl.CostEstimate(
             flops=2 * hh * toks * dqk * dv, bytes_accessed=11 * 1024 * 1024, transcendentals=0),
         name="readout",

time: 50.1 us -> 48.9 us (0.976)
  Pallas kernels: 49.2 us -> 45.9 us
  local copies, waits for them, and re-layouts: 0 us -> 2.18 us
    pallas_call x1, Pallas kernels: 8.27 us -> 5.38 us  [on_device(): pl.pallas_call(functools.partial(readout, hh, dv // CW), grid=(toks // tb...]
    unnamed x0 -> x6, local copies, waits for them, and re-layouts: none -> 2.18 us
where the time goes in v3:
time: 48.9 us; the launch traced here: 48.7 us
  Pallas kernels  45.9 us (94%)
  local copies, waits for them, and re-layouts  2.18 us (4%)
  between operations  0.65 us (1%)
    pallas_call x1, Pallas kernels, on_device(): pl.pallas_call(functools.partial(kernel, nc, nh, hh, toks, dqk, dv), out_...  40.5 us
    pallas_call x1, Pallas kernels, on_device(): pl.pallas_call(functools.partial(readout, hh, dv // CW), grid=(toks // tb...  5.38 us
    unnamed x6, local copies, waits for them, and re-layouts  2.18 us

profile of v3, /device:TPU:0, one launch (start us, length us, event | category | flops | bytes accessed | tf_op | source)
XLA Modules:
  0.0 48.7 jit_solution(4549597334632399196)
XLA Ops:
  0.6 40.5 %mlstm.1 = (bf16[2,2048,512]{2,1,0:T(8,128)(2,1)S(1)}, bf16[2,2048,256]{2,1,0:T(8,128)(2,1)S(1)}, bf16[8,256,128]{2,1,0:T(8,128)(2,1)S(1)}, f32[2,32,512]{2,1,0:...) custom-call(bf16[2048,512]{1,0:T(8,128)(2,1)} %q_hbm.1, bf16[2048,512]{1,0:T(8,128)(2,1)} %k_hbm.1, ...), custom_call_target="tpu_custom_call" | custom-call | flops 6442450944 | bytes 12582912 | tf_op jit(solution)/shard_map/mlstm/pallas_call | solution.py:422
  41.1 0.0 copy-start
  41.1 0.9 %copy-done = f32[2,32,512]{2,1,0:T(8,128)S(1)} copy-done((f32[2,32,512]{2,1,0:T(8,128)S(1)}, f32[2,32,512]{2,1,0:T(8,128)}, u32[]{:S(2)}) %copy-start) | copy-done | bytes 131096
  42.0 0.0 copy-start.1
  42.0 0.7 %copy-done.1 = f32[2,256]{1,0:T(2,128)S(1)} copy-done((f32[2,256]{1,0:T(2,128)S(1)}, f32[2,256]{1,0:T(2,128)}, u32[]{:S(2)}) %copy-start.1) | copy-done | bytes 2072
  42.7 0.0 copy-start.2
  42.7 0.6 %copy-done.2 = f32[2,128]{1,0:T(2,128)S(1)} copy-done((f32[2,128]{1,0:T(2,128)S(1)}, f32[2,128]{1,0:T(2,128)}, u32[]{:S(2)}) %copy-start.2) | copy-done | bytes 1048
  43.3 5.4 %readout.1 = (bf16[2048,1024]{1,0:T(8,128)(2,1)}, f32[2,32,512]{2,1,0:T(8,128)}, f32[2,256]{1,0:T(2,128)}, f32[2]{0:T(128)}) custom-call(bf16[2,2048,512]{2,1,0:T(8,128)(2,1)S(1)} %get-tuple-element.10.num_ref, bf16[2,2048,256]{2,1,0:T(8,128)(2,1)S(1)} %get-tuple-element.11.qs_ref, bf16[8,256,128]{2,1,0:T(8,128)(2,1)S(1)} %get-tuple-element.12.mem_ref, ...), custom_call_target="tpu_custom_call" | custom-call | flops 1073741824 | bytes 11534336 | tf_op jit(solution)/shard_map/readout/pallas_call | solution.py:460
Async XLA Ops:
  41.1 0.9 %copy-start = (f32[2,32,512]{2,1,0:T(8,128)S(1)}, f32[2,32,512]{2,1,0:T(8,128)}, u32[]{:S(2)}) copy-start(f32[2,32,512]{2,1,0:T(8,128)} %get-tuple-element.13.clos_in) | copy-start | bytes 393220
  42.0 0.7 %copy-start.1 = (f32[2,256]{1,0:T(2,128)S(1)}, f32[2,256]{1,0:T(2,128)}, u32[]{:S(2)}) copy-start(f32[2,256]{1,0:T(2,128)} %get-tuple-element.14.norm_in) | copy-start | bytes 6148
  42.7 0.6 %copy-start.2 = (f32[2,128]{1,0:T(2,128)S(1)}, f32[2,128]{1,0:T(2,128)}, u32[]{:S(2)}) copy-start(f32[2,128]{1,0:T(2,128)} %get-tuple-element.15.max_in) | copy-start | bytes 3076

commit v4 on v3

--- a/solution.py
+++ b/solution.py
@@ -53,7 +53,6 @@
         loads.append((kc, vc, qc))
     for h in range(hh):
         loads[h][0].start()
-        loads[h][1].start()
 
     barrier = pltpu.get_barrier_semaphore()
     for d in range(1, nh):
@@ -64,6 +63,8 @@
     for p in range(nh):
         gsend[p, 0:hh, :] = g_v[0, p * hh:(p + 1) * hh, :]
         gsend[p, hh:2 * hh, :] = g_v[1, p * hh:(p + 1) * hh, :]
+    for h in range(hh):
+        loads[h][1].start()
     pl.semaphore_wait(barrier, nh - 1 + nc - 1)
 
     def gate_copy(d):
@@ -398,7 +399,7 @@
         clos_out[...] = clos_in[...]
         norm_out[...] = norm_in[...]
         for h in range(hh):
-            max_out[h] = max_in[h, 0]
+            max_out[h] = jnp.max(max_in[h:h + 1, :])
 
 
 def on_device(nc, nh, queries, keys, values, gate_pre):
@@ -425,9 +426,9 @@
             vm((hh, toks, dv), BF16),
             vm((hh, toks, dqk), BF16),
             vm((nu, dqk, CW), BF16),
-            jax.ShapeDtypeStruct((hh, R, dv), F32),
-            jax.ShapeDtypeStruct((hh, dqk), F32),
-            jax.ShapeDtypeStruct((hh, 128), F32),
+            vm((hh, R, dv), F32),
+            vm((hh, dqk), F32),
+            vm((hh, 128), F32),
         ),
         in_specs=[anyspec] * 4,
         out_specs=(vspec,) * 6,
@@ -453,10 +454,10 @@
             flops=2 * macs, bytes_accessed=12 * 1024 * 1024, transcendentals=hh * toks * L),
         name="mlstm",
     )(queries, keys, values, gate_pre)
-    tb = min(256, toks)
-    num = pltpu.with_memory_space_constraint(num, pltpu.VMEM)
-    qs = pltpu.with_memory_space_constraint(qs, pltpu.VMEM)
-    mem = pltpu.with_memory_space_constraint(mem, pltpu.VMEM)
+    tb = min(512, toks)
+    num, qs, mem, closing, norm, top = (
+        pltpu.with_memory_space_constraint(t, pltpu.VMEM)
+        for t in (num, qs, mem, closing, norm, top))
     return pl.pallas_call(
         functools.partial(readout, hh, dv // CW),
         grid=(toks // tb,),
@@ -467,7 +468,7 @@
             jax.ShapeDtypeStruct((hh,), F32),
         ),
         in_specs=[
-            vspec, vspec, vspec, vspec, vspec, pl.BlockSpec(memory_space=pltpu.SMEM),
+            vspec, vspec, vspec, vspec, vspec, vspec,
         ],
         out_specs=(
             pl.BlockSpec((tb, hh * dv), lambda t: (t, 0)),

time: 48.9 us -> 44.1 us (0.902)
  Pallas kernels: 45.9 us -> 43.3 us
  local copies, waits for them, and re-layouts: 2.18 us -> 0 us
    unnamed x6 -> x0, local copies, waits for them, and re-layouts: 2.18 us -> none
    pallas_call x1, Pallas kernels: 5.38 us -> 3.5 us  [on_device(): pl.pallas_call(functools.partial(readout, hh, dv // CW), grid=(toks // tb...]
    pallas_call x1, Pallas kernels: 40.5 us -> 39.8 us  [on_device(): pl.pallas_call(functools.partial(kernel, nc, nh, hh, toks, dqk, dv), out_...]
where the time goes in v4:
time: 44.1 us; the launch traced here: 44 us
  Pallas kernels  43.3 us (98%)
  between operations  0.64 us (1%)
    pallas_call x1, Pallas kernels, on_device(): pl.pallas_call(functools.partial(kernel, nc, nh, hh, toks, dqk, dv), out_...  39.8 us
    pallas_call x1, Pallas kernels, on_device(): pl.pallas_call(functools.partial(readout, hh, dv // CW), grid=(toks // tb...  3.5 us

profile of v4, /device:TPU:0, one launch (start us, length us, event | category | flops | bytes accessed | tf_op | source)
XLA Modules:
  0.0 44.0 jit_solution(3421265265322759538)
XLA Ops:
  0.6 39.8 %mlstm.1 = (bf16[2,2048,512]{2,1,0:T(8,128)(2,1)S(1)}, bf16[2,2048,256]{2,1,0:T(8,128)(2,1)S(1)}, bf16[8,256,128]{2,1,0:T(8,128)(2,1)S(1)}, f32[2,32,512]{2,1,0:...) custom-call(bf16[2048,512]{1,0:T(8,128)(2,1)} %q_hbm.1, bf16[2048,512]{1,0:T(8,128)(2,1)} %k_hbm.1, ...), custom_call_target="tpu_custom_call" | custom-call | flops 6442450944 | bytes 12582912 | tf_op jit(solution)/shard_map/mlstm/pallas_call | solution.py:423
  40.5 3.5 %readout.1 = (bf16[2048,1024]{1,0:T(8,128)(2,1)}, f32[2,32,512]{2,1,0:T(8,128)}, f32[2,256]{1,0:T(2,128)}, f32[2]{0:T(128)}) custom-call(bf16[2,2048,512]{2,1,0:T(8,128)(2,1)S(1)} %get-tuple-element.10.num_ref, bf16[2,2048,256]{2,1,0:T(8,128)(2,1)S(1)} %get-tuple-element.11.qs_ref, bf16[8,256,128]{2,1,0:T(8,128)(2,1)S(1)} %get-tuple-element.12.mem_ref, ...), custom_call_target="tpu_custom_call" | custom-call | flops 1073741824 | bytes 11534336 | tf_op jit(solution)/shard_map/readout/pallas_call | solution.py:461
